TPU v7x, 32 devices: a whole 2x2x4 slice. The times are simulated.
32 devices in a mesh: expert: 16 (over z, y, core), dp: 2 (over x).
Axes of the slice: x: 2, y: 2, z: 4, core: 2. Of those that a mesh axis runs over, the one named last changes fastest.
Arguments:
- activations: bfloat16 [512, 7168], P(('expert', 'dp')), may hold values from -6 to 6
- cotangent: bfloat16 [512, 7168], P(('expert', 'dp')), may hold values from -6 to 6
- route_ids: int32 [512, 8], P(('expert', 'dp')), may hold values from 0 to 15, all different within a row; in each aligned block of 16 rows (0 to 15, 16 to 31, ...) at most 10 rows name the same one
- route_weights: float32 [512, 8], P(('expert', 'dp')), may hold values from 0.05 to 0.6
- gate_weights: bfloat16 [16, 7168, 1024], P('expert', 'dp'), may hold values from -0.0625 to 0.0625
- up_weights: bfloat16 [16, 7168, 1024], P('expert', 'dp'), may hold values from -0.0625 to 0.0625
- down_weights: bfloat16 [16, 1024, 7168], P('expert', None, 'dp'), may hold values from -0.1875 to 0.1875
Outputs:
- grad_input: bfloat16 [512, 7168], P(('expert', 'dp'))
- grad_gate: bfloat16 [16, 7168, 1024], P('expert', 'dp')
- grad_up: bfloat16 [16, 7168, 1024], P('expert', 'dp')
- grad_down: bfloat16 [16, 1024, 7168], P('expert', None, 'dp')
Inputs may be any that keep to these rules, and one draw needn't show every extreme that they name: `route_ids`: each token names 8 different experts. Among the routes of one device's 16 tokens, no expert is named more than 10 times, a bound that some block reaches.
All inputs are finite; a program needn't handle non-finite values.
Results may differ from a plain program's by a relative error of at most 0.0064.
Values may be sent and summed in bfloat16 or wider, within the bound.
A program may use at most 128 MiB of HBM per device.

v0:
```python
import jax
import jax.numpy as jnp
from jax import lax
from jax.sharding import PartitionSpec as P


def swiglu_back(gate, upper, upstream):
    sigma = jax.nn.sigmoid(gate)
    silu_gate = gate * sigma
    activated = (silu_gate * upper).astype(jnp.bfloat16)
    grad_pre = (upstream * upper * sigma * (1.0 + gate * (1.0 - sigma))).astype(jnp.bfloat16)
    grad_lin = (upstream * silu_gate).astype(jnp.bfloat16)
    return (grad_pre, grad_lin, activated)


def contract_rows(left, right):
    return lax.dot_general(
        left, right, (((0,), (0,)), ((), ())), preferred_element_type=jnp.float32
    )


def shards(
    activations, cotangent, route_ids, route_weights, gate_weights, up_weights, down_weights
):
    tok_rows, width = activations.shape
    topk = route_ids.shape[1]
    num_dp = lax.axis_size("dp")
    num_exp = lax.axis_size("expert")
    slice_width = gate_weights.shape[1]
    hidden = gate_weights.shape[2]
    capacity = min(tok_rows, 5 * tok_rows * topk // (4 * num_exp))
    buffer_rows = num_exp * num_dp * capacity
    flat_ids = route_ids.reshape(-1)
    expert_iota = jnp.arange(num_exp, dtype=jnp.int32)
    onehot = (flat_ids[:, None] == expert_iota[None, :]).astype(jnp.int32)
    before = jnp.cumsum(onehot, axis=0) - onehot
    slot = jnp.sum(before * onehot, axis=1)
    target = (flat_ids * capacity + slot).reshape(tok_rows, topk)
    slot_iota = jnp.arange(num_exp * capacity, dtype=jnp.int32)
    matches = target[:, :, None] == slot_iota[None, None, :]
    placing = jnp.any(matches, axis=1).astype(jnp.bfloat16)
    slot_weight = jnp.sum(jnp.where(matches, route_weights[:, :, None], 0.0), axis=(0, 1))
    send_act = contract_rows(placing, activations).astype(jnp.bfloat16)
    send_cot = (contract_rows(placing, cotangent) * slot_weight[:, None]).astype(jnp.bfloat16)
    send_act = send_act.reshape(num_exp, capacity, num_dp, slice_width)
    send_cot = send_cot.reshape(num_exp, capacity, num_dp, slice_width)
    flat_act = jnp.swapaxes(send_act, 1, 2).reshape(num_exp * num_dp, capacity, slice_width)
    flat_cot = jnp.swapaxes(send_cot, 1, 2).reshape(num_exp * num_dp, capacity, slice_width)
    recv_act, recv_cot = (
        lax.all_to_all(flat_act, ("expert", "dp"), split_axis=0, concat_axis=0, tiled=True),
        lax.all_to_all(flat_cot, ("expert", "dp"), split_axis=0, concat_axis=0, tiled=True),
    )
    recv_act = recv_act.reshape(buffer_rows, slice_width)
    recv_cot = recv_cot.reshape(buffer_rows, slice_width)
    gate_local = gate_weights[0]
    up_local = up_weights[0]
    down_local = down_weights[0]
    act_rows = recv_act
    cot_rows = recv_cot
    gate_part = jnp.dot(act_rows, gate_local, preferred_element_type=jnp.float32)
    up_part = jnp.dot(act_rows, up_local, preferred_element_type=jnp.float32)
    back_part = lax.dot_general(
        cot_rows, down_local, (((1,), (1,)), ((), ())), preferred_element_type=jnp.float32
    )
    summed = lax.psum(jnp.concatenate([gate_part, up_part, back_part], axis=1), "dp")
    grad_pre, grad_lin, activated = swiglu_back(
        summed[:, :hidden], summed[:, hidden : 2 * hidden], summed[:, 2 * hidden :]
    )
    act_rows = recv_act
    cot_rows = recv_cot
    rows_back = lax.dot_general(
        grad_pre, gate_local, (((1,), (1,)), ((), ())), preferred_element_type=jnp.float32
    ) + lax.dot_general(
        grad_lin, up_local, (((1,), (1,)), ((), ())), preferred_element_type=jnp.float32
    )
    grad_gate = contract_rows(act_rows, grad_pre).astype(jnp.bfloat16)[None]
    grad_up = contract_rows(act_rows, grad_lin).astype(jnp.bfloat16)[None]
    grad_down = contract_rows(activated, cot_rows).astype(jnp.bfloat16)[None]
    back_rows = rows_back.astype(jnp.bfloat16)
    flat_back = back_rows.reshape(num_exp * num_dp, capacity, slice_width)
    arrived = lax.all_to_all(flat_back, ("expert", "dp"), split_axis=0, concat_axis=0, tiled=True)
    arrived = jnp.swapaxes(arrived.reshape(num_exp, num_dp, capacity, slice_width), 1, 2)
    arrived = arrived.reshape(num_exp * capacity, width)
    grad_input = jnp.dot(placing, arrived, preferred_element_type=jnp.float32).astype(jnp.bfloat16)
    return (grad_input, grad_gate, grad_up, grad_down)


def solution(mesh):
    placed = (
        P(("expert", "dp"), None),
        P(("expert", "dp"), None),
        P(("expert", "dp"), None),
        P(("expert", "dp"), None),
        P("expert", "dp", None),
        P("expert", "dp", None),
        P("expert", None, "dp"),
    )
    return jax.shard_map(
        shards,
        mesh=mesh,
        in_specs=placed,
        out_specs=(
            P(("expert", "dp"), None),
            P("expert", "dp", None),
            P("expert", "dp", None),
            P("expert", None, "dp"),
        ),
        check_vma=False,
    )
```

profile of v0, /device:TPU:0, one launch (start us, length us, event | category | flops | bytes accessed | tf_op | source)
XLA Modules:
  0.0 427.5 jit_solution(12015261258856971701)
XLA Ops:
  7.2 0.8 copy.30
  8.2 0.2 reduce_window_sum.11
  8.8 2.2 convolution_convert_fusion
  10.9 3.4 reshape.45
  14.4 2.4 copy.38
  16.8 7.4 %all-to-all-start = ((bf16[32,10,3584]{2,1,0:T(8,128)(2,1)}), bf16[32,10,3584]{2,1,0:T(8,128)(2,1)}, u32[]{:S(2)}, u32[]{:S(2)}) async-start(bf16[32,10,3584]{2,1,0:T(8,128)(2,1)} %bitcast.51), calls=%async_computation | async-start | bytes 7340032 | tf_op jit(solution)/shard_map/all_to_all | solution.py:50
  24.4 0.8 fusion
  25.2 2.9 reshape.48
  28.1 4.0 copy.39
  32.2 74.5 %all-to-all-done = bf16[32,10,3584]{2,1,0:T(8,128)(2,1)} async-done(((bf16[32,10,3584]{2,1,0:T(8,128)(2,1)}), bf16[32,10,3584]{2,1,0:T(8,128)(2,1)}, u32[]{:S(2)}, u32[]{:S(2)}) %all-to-all-start) | async-done | bytes 2293792 | tf_op jit(solution)/shard_map/all_to_all | solution.py:50
  106.7 4.5 %all-to-all-start.1 = ((bf16[32,10,3584]{2,1,0:T(8,128)(2,1)}), bf16[32,10,3584]{2,1,0:T(8,128)(2,1)}, u32[]{:S(2)}, u32[]{:S(2)}) async-start(bf16[32,10,3584]{2,1,0:T(8,128)(2,1)} %bitcast.50), calls=%async_computation.1 | async-start | bytes 7340032 | tf_op jit(solution)/shard_map/all_to_all | solution.py:51
  111.2 0.2 all-reduce.2.cloned.1.call-start
  111.5 3.1 reshape.47
  114.6 6.7 %fusion.5 = f32[320,1024]{1,0:T(8,128)} fusion(bf16[320,3584]{1,0:T(8,128)(2,1)S(1)} %reshape.47, bf16[1,3584,1024]{2,1,0:T(8,128)(2,1)} %param.12), kind=kOutput, calls=%fused_computation.11 | convolution fusion | flops 2348810240 | bytes 10944512 | tf_op jit(solution)/shard_map/dot_general | solution.py:61
  121.3 6.7 %fusion.9 = f32[320,1024]{1,0:T(8,128)} fusion(bf16[320,3584]{1,0:T(8,128)(2,1)S(1)} %reshape.47, bf16[1,3584,1024]{2,1,0:T(8,128)(2,1)} %param.11), kind=kOutput, calls=%fused_computation.15 | convolution fusion | flops 2348810240 | bytes 10944512 | tf_op jit(solution)/shard_map/dot_general | solution.py:60
  127.9 65.8 %all-to-all-done.1 = bf16[32,10,3584]{2,1,0:T(8,128)(2,1)} async-done(((bf16[32,10,3584]{2,1,0:T(8,128)(2,1)}), bf16[32,10,3584]{2,1,0:T(8,128)(2,1)}, u32[]{:S(2)}, u32[]{:S(2)}) %all-to-all-start.1) | async-done | bytes 2293792 | tf_op jit(solution)/shard_map/all_to_all | solution.py:51
  193.7 4.5 %reshape.50 = bf16[320,3584]{1,0:T(8,128)(2,1)} reshape(bf16[32,10,3584]{2,1,0:T(8,128)(2,1)} %all-to-all-done.1) | data formatting | bytes 4587520 | tf_op jit(solution)/shard_map/reshape | solution.py:54
  198.2 6.5 %fusion.1 = f32[320,1024]{1,0:T(8,128)S(1)} fusion(bf16[320,3584]{1,0:T(8,128)(2,1)} %reshape.50, bf16[1,1024,3584]{2,1,0:T(8,128)(2,1)} %param.13), kind=kOutput, calls=%fused_computation.7 | convolution fusion | flops 2348810240 | bytes 10944512 | tf_op jit(solution)/shard_map/dot_general | solution.py:62
  204.7 2.4 pad_maximum_fusion
  207.1 102.9 %all-reduce.2.cloned.1.call-done = f32[320,3072]{1,0:T(8,128)} async-done(((f32[320,3072]{1,0:T(8,128)}), f32[320,3072]{1,0:T(8,128)}) %all-reduce.2.cloned.1.call-update) | async-done | bytes 3932176 | tf_op jit(solution)/shard_map/psum | solution.py:65
  310.0 3.1 multiply_convert_fusion.2
  313.1 5.9 %fusion.3 = f32[320,3584]{1,0:T(8,128)S(1)} fusion(bf16[320,1024]{1,0:T(8,128)(2,1)S(1)} %get-tuple-element.5, bf16[1,3584,1024]{2,1,0:T(8,128)(2,1)} %param.12), kind=kOutput, calls=%fused_computation.9 | convolution fusion | flops 2348810240 | bytes 12582912 | tf_op jit(solution)/shard_map/dot_general | solution.py:73
  319.1 4.0 fusion.17
  323.1 4.4 %reshape.51 = bf16[32,10,3584]{2,1,0:T(8,128)(2,1)} reshape(bf16[320,3584]{1,0:T(8,128)(2,1)} %fusion.17) | data formatting | bytes 4587520 | tf_op jit(solution)/shard_map/reshape | solution.py:80
  327.5 4.9 %all-to-all-start.2 = ((bf16[32,10,3584]{2,1,0:T(8,128)(2,1)}), bf16[32,10,3584]{2,1,0:T(8,128)(2,1)}, u32[]{:S(2)}, u32[]{:S(2)}) async-start(bf16[32,10,3584]{2,1,0:T(8,128)(2,1)} %reshape.51), calls=%async_computation.2 | async-start | bytes 7340032 | tf_op jit(solution)/shard_map/all_to_all | solution.py:81
  332.4 7.2 %fusion.11 = bf16[1,3584,1024]{2,1,0:T(8,128)(2,1)} fusion(bf16[320,3584]{1,0:T(8,128)(2,1)S(1)} %reshape.47, bf16[320,1024]{1,0:T(8,128)(2,1)} %copy-done.5), kind=kOutput, calls=%fused_computation.17 | convolution fusion | flops 2352480256 | bytes 10289152 | tf_op jit(solution)/shard_map/dot_general | solution.py:17
  339.6 6.1 %fusion.12 = bf16[1,3584,1024]{2,1,0:T(8,128)(2,1)} fusion(bf16[320,3584]{1,0:T(8,128)(2,1)S(1)} %reshape.47, bf16[320,1024]{1,0:T(8,128)(2,1)S(1)} %get-tuple-element.5), kind=kOutput, calls=%fused_computation.18 | convolution fusion | flops 2352480256 | bytes 10289152 | tf_op jit(solution)/shard_map/dot_general | solution.py:17
  345.7 7.9 %fusion.13 = bf16[1,1024,3584]{2,1,0:T(8,128)(2,1)} fusion(bf16[320,3584]{1,0:T(8,128)(2,1)S(1)} %copy-done.2, f32[320,3072]{1,0:T(8,128)} %all-reduce.2.cloned.1.call-done), kind=kOutput, calls=%fused_computation.19 | convolution fusion | flops 2354446336 | bytes 12255232 | tf_op jit(solution)/shard_map/dot_general | solution.py:17
  353.6 61.2 %all-to-all-done.2 = bf16[32,10,3584]{2,1,0:T(8,128)(2,1)} async-done(((bf16[32,10,3584]{2,1,0:T(8,128)(2,1)}), bf16[32,10,3584]{2,1,0:T(8,128)(2,1)}, u32[]{:S(2)}, u32[]{:S(2)}) %all-to-all-start.2) | async-done | bytes 2293792 | tf_op jit(solution)/shard_map/all_to_all | solution.py:81
  414.8 4.4 %copy.37 = bf16[16,2,10,3584]{3,1,2,0:T(2,128)(2,1)S(1)} copy(bf16[16,2,10,3584]{3,2,1,0:T(8,128)(2,1)} %bitcast.7) | data formatting | bytes 4587520 | tf_op jit(solution)/shard_map/reshape | solution.py:82
  419.2 0.3 copy.42
  419.5 1.1 convolution_convert_fusion.1
  (30 shorter events, 0.8 us)
Async XLA Ops:
  7.2 1.6 copy-start
  16.8 7.4 %copy-start.7 = (f32[16,8]{0,1:T(8,128)S(1)}, f32[16,8]{0,1:T(8,128)}, u32[]{:S(2)}) copy-start(f32[16,8]{0,1:T(8,128)} %param.10) | copy-start | bytes 1540
  16.8 7.6 %copy-start.6 = (bf16[16,7168]{1,0:T(8,128)(2,1)S(1)}, bf16[16,7168]{1,0:T(8,128)(2,1)}, u32[]{:S(2)}) copy-start(bf16[16,7168]{1,0:T(8,128)(2,1)} %param.8) | copy-start | bytes 688132
  16.8 89.9 %all-to-all-start = ((bf16[32,10,3584]{2,1,0:T(8,128)(2,1)}), bf16[32,10,3584]{2,1,0:T(8,128)(2,1)}, u32[]{:S(2)}, u32[]{:S(2)}) async-start(bf16[32,10,3584]{2,1,0:T(8,128)(2,1)} %bitcast.51), calls=%async_computation | async-start | bytes 7340032 | tf_op jit(solution)/shard_map/all_to_all | solution.py:50
  106.7 87.0 %all-to-all-start.1 = ((bf16[32,10,3584]{2,1,0:T(8,128)(2,1)}), bf16[32,10,3584]{2,1,0:T(8,128)(2,1)}, u32[]{:S(2)}, u32[]{:S(2)}) async-start(bf16[32,10,3584]{2,1,0:T(8,128)(2,1)} %bitcast.50), calls=%async_computation.1 | async-start | bytes 7340032 | tf_op jit(solution)/shard_map/all_to_all | solution.py:51
  111.2 198.7 %all-reduce.2.cloned.1.call-start = ((), (), s32[]{:S(2)}) async-start(), calls=%async_computation.3 | async-start | bytes 7864320 | tf_op jit(solution)/shard_map/psum | solution.py:65
  198.2 6.5 %copy-start.3 = (f32[320,1024]{1,0:T(8,128)S(1)}, f32[320,1024]{1,0:T(8,128)}, u32[]{:S(2)}) copy-start(f32[320,1024]{1,0:T(8,128)} %fusion.5) | copy-start | bytes 3932164
  198.2 6.5 %copy-start.4 = (f32[320,1024]{1,0:T(8,128)S(1)}, f32[320,1024]{1,0:T(8,128)}, u32[]{:S(2)}) copy-start(f32[320,1024]{1,0:T(8,128)} %fusion.9) | copy-start | bytes 3932164
  310.0 9.0 %slice-start = ((s8[7340032]{0:T(1024)(128)(4,1)}), s8[4194304]{0:T(1024)(128)(4,1)S(1)}, s32[]{:S(2)}) async-start(s8[7340032]{0:T(1024)(128)(4,1)} %bitcast.56), calls=%async_computation.4 | async-start | bytes 8388608
  313.1 6.0 %copy-start.5 = (bf16[320,1024]{1,0:T(8,128)(2,1)}, bf16[320,1024]{1,0:T(8,128)(2,1)S(1)}, u32[]{:S(2)}) copy-start(bf16[320,1024]{1,0:T(8,128)(2,1)S(1)} %get-tuple-element.4) | copy-start | bytes 1966084
  313.1 6.0 %slice-start.1 = ((s8[7340032]{0:T(1024)(128)(4,1)}), s8[3145728]{0:T(1024)(128)(4,1)S(1)}, s32[]{:S(2)}) async-start(s8[7340032]{0:T(1024)(128)(4,1)} %bitcast.56), calls=%async_computation.5 | async-start | bytes 6291456
  327.5 87.3 %all-to-all-start.2 = ((bf16[32,10,3584]{2,1,0:T(8,128)(2,1)}), bf16[32,10,3584]{2,1,0:T(8,128)(2,1)}, u32[]{:S(2)}, u32[]{:S(2)}) async-start(bf16[32,10,3584]{2,1,0:T(8,128)(2,1)} %reshape.51), calls=%async_computation.2 | async-start | bytes 7340032 | tf_op jit(solution)/shard_map/all_to_all | solution.py:81
  339.6 6.1 %copy-start.2 = (bf16[320,3584]{1,0:T(8,128)(2,1)S(1)}, bf16[320,3584]{1,0:T(8,128)(2,1)}, u32[]{:S(2)}) copy-start(bf16[320,3584]{1,0:T(8,128)(2,1)} %reshape.50) | copy-start | bytes 6881284
  419.2 1.4 copy-start.1
Sparse Core Ops, SparseCore 0:
  207.2 102.7 all-reduce.1
where the time goes:
time: 428 us; the launch traced here: 427 us
  waiting for transfers between devices  304 us (71%)
  matrix products  55 us (13%)
  local copies, waits for them, and re-layouts  30.6 us (7%)
  starting transfers between devices  17.1 us (4%)
  between operations  14.3 us (3%)
  other arithmetic  6.11 us (1%)
    psum x1, waiting for transfers between devices, shards(): lax.psum(jnp.concatenate([gate_part, up_part, back_part], axis=1), 'dp')  103 us
    all_to_all x1, waiting for transfers between devices, shards(): lax.all_to_all(flat_act, ('expert', 'dp'), split_axis=0, concat_axis=0, t...  74.5 us
    all_to_all x1, waiting for transfers between devices, shards(): lax.all_to_all(flat_cot, ('expert', 'dp'), split_axis=0, concat_axis=0, t...  65.8 us
    all_to_all x1, waiting for transfers between devices, shards(): lax.all_to_all(flat_back, ('expert', 'dp'), split_axis=0, concat_axis=0,...  61.2 us
    dot_general x5, matrix products, contract_rows(): lax.dot_general(left, right, (((0,), (0,)), ((), ())), preferred_element_...  24.2 us
  transfers between devices with their start and end apart: 4, of which 4 were waited for; matrix products, arithmetic and copies ran while one was open for 11% of the time, Pallas kernels for 0%

commit v1 on v0

v1 whole, which is shorter than its diff:
```python
import jax
import jax.numpy as jnp
from jax import lax
from jax.sharding import PartitionSpec as P


def swiglu_back(gate, upper, upstream):
    sigma = jax.nn.sigmoid(gate)
    silu_gate = gate * sigma
    activated = (silu_gate * upper).astype(jnp.bfloat16)
    grad_pre = (upstream * upper * sigma * (1.0 + gate * (1.0 - sigma))).astype(jnp.bfloat16)
    grad_lin = (upstream * silu_gate).astype(jnp.bfloat16)
    return (grad_pre, grad_lin, activated)


def contract_rows(left, right):
    return lax.dot_general(
        left, right, (((0,), (0,)), ((), ())), preferred_element_type=jnp.float32
    )


def contract_last(left, right):
    return lax.dot_general(
        left, right, (((1,), (1,)), ((), ())), preferred_element_type=jnp.float32
    )


def to_slices(block, num_dp):
    rows, width = block.shape
    pieces = jnp.swapaxes(block.reshape(rows, num_dp, width // num_dp), 0, 1)
    return lax.all_to_all(pieces, "dp", split_axis=0, concat_axis=0, tiled=True)


def dp_total(part, num_dp):
    sent = part.astype(jnp.bfloat16)
    total = part
    for shift in range(1, num_dp):
        got = lax.ppermute(sent, "dp", [(i, (i + shift) % num_dp) for i in range(num_dp)])
        total = total + got.astype(jnp.float32)
    return total


def placement(ids, weights, capacity, tok_rows, expert):
    tokens, topk = ids.shape
    blocks = tokens // tok_rows
    named = ids == expert
    hit = jnp.any(named, axis=1).reshape(blocks, tok_rows)
    weight = jnp.sum(jnp.where(named, weights, 0.0), axis=1)
    hit_int = hit.astype(jnp.int32)
    earlier = jnp.cumsum(hit_int, axis=1) - hit_int
    row = jnp.arange(blocks, dtype=jnp.int32)[:, None] * capacity + earlier
    row = jnp.where(hit, row, -1).reshape(tokens)
    row_iota = jnp.arange(blocks * capacity, dtype=jnp.int32)
    matches = row[None, :] == row_iota[:, None]
    row_weight = jnp.sum(jnp.where(matches, weight[None, :], 0.0), axis=1)
    return matches.astype(jnp.bfloat16), row_weight


def shards(
    activations, cotangent, route_ids, route_weights, gate_weights, up_weights, down_weights
):
    tok_rows, width = activations.shape
    topk = route_ids.shape[1]
    num_dp = lax.axis_size("dp")
    num_exp = lax.axis_size("expert")
    slice_width = gate_weights.shape[1]
    tokens = tok_rows * num_exp * num_dp
    capacity = min(tok_rows, 5 * tok_rows * topk // (4 * num_exp))
    routing = jnp.concatenate([route_ids.astype(jnp.float32), route_weights], axis=1)
    routing = lax.all_gather(routing, ("expert", "dp"), axis=0, tiled=True)
    all_act = lax.all_gather(to_slices(activations, num_dp), "expert", axis=0, tiled=True)
    all_cot = lax.all_gather(to_slices(cotangent, num_dp), "expert", axis=0, tiled=True)
    all_act = all_act.reshape(tokens, slice_width)
    all_cot = all_cot.reshape(tokens, slice_width)
    placing, row_weight = placement(
        routing[:, :topk].astype(jnp.int32),
        routing[:, topk:],
        capacity,
        tok_rows,
        lax.axis_index("expert"),
    )
    gate_local = gate_weights[0]
    up_local = up_weights[0]
    down_local = down_weights[0]
    act_rows = jnp.dot(placing, all_act, preferred_element_type=jnp.float32).astype(jnp.bfloat16)
    gate = dp_total(jnp.dot(act_rows, gate_local, preferred_element_type=jnp.float32), num_dp)
    upper = dp_total(jnp.dot(act_rows, up_local, preferred_element_type=jnp.float32), num_dp)
    cot_rows = jnp.dot(placing, all_cot, preferred_element_type=jnp.float32)
    cot_rows = (cot_rows * row_weight[:, None]).astype(jnp.bfloat16)
    upstream = dp_total(contract_last(cot_rows, down_local), num_dp)
    grad_pre, grad_lin, activated = swiglu_back(gate, upper, upstream)
    rows_back = contract_last(grad_pre, gate_local) + contract_last(grad_lin, up_local)
    rows_back = rows_back.astype(jnp.bfloat16)
    tokens_back = contract_rows(placing, rows_back).astype(jnp.bfloat16)
    arrived = lax.psum_scatter(tokens_back, "expert", scatter_dimension=0, tiled=True)
    grad_gate = contract_rows(act_rows, grad_pre).astype(jnp.bfloat16)[None]
    grad_up = contract_rows(act_rows, grad_lin).astype(jnp.bfloat16)[None]
    grad_down = contract_rows(activated, cot_rows).astype(jnp.bfloat16)[None]
    arrived = arrived.reshape(num_dp, tok_rows, slice_width)
    arrived = lax.all_to_all(arrived, "dp", split_axis=0, concat_axis=0, tiled=True)
    grad_input = jnp.swapaxes(arrived, 0, 1).reshape(tok_rows, width)
    return (grad_input, grad_gate, grad_up, grad_down)


def solution(mesh):
    placed = (
        P(("expert", "dp"), None),
        P(("expert", "dp"), None),
        P(("expert", "dp"), None),
        P(("expert", "dp"), None),
        P("expert", "dp", None),
        P("expert", "dp", None),
        P("expert", None, "dp"),
    )
    return jax.shard_map(
        shards,
        mesh=mesh,
        in_specs=placed,
        out_specs=(
            P(("expert", "dp"), None),
            P("expert", "dp", None),
            P("expert", "dp", None),
            P("expert", None, "dp"),
        ),
        check_vma=False,
    )
```

time: 428 us -> 276 us (0.64)
  waiting for transfers between devices: 304 us -> 104 us
  blocking collectives: 0 us -> 85 us
  local copies, waits for them, and re-layouts: 30.6 us -> 3.42 us
  starting transfers between devices: 17.1 us -> 7.47 us
  matrix products: 55 us -> 60 us
    all_to_all x3 -> x1, waiting for transfers between devices: 202 us -> 0.01 us  [shards(): lax.all_to_all(arrived, 'dp', split_axis=0, concat_axis=0, tiled=True)]
    psum x1 -> x0, waiting for transfers between devices: 103 us -> none  [shards(): lax.psum(jnp.concatenate([gate_part, up_part, back_part], axis=1), 'dp')]
    all_gather x0 -> x1, blocking collectives: none -> 67.5 us  [shards(): routing = lax.all_gather(routing, ('expert', 'dp'), axis=0, tiled=True)]
    reduce_scatter x0 -> x1, waiting for transfers between devices: none -> 52.5 us  [shards(): lax.psum_scatter(tokens_back, 'expert', scatter_dimension=0, tiled=True)]
    ppermute x0 -> x3, waiting for transfers between devices: none -> 36.3 us  [dp_total(): lax.ppermute(sent, 'dp', [(i, (i + shift) % num_dp) for i in range(num_dp)])]
    reshape x8 -> x3, local copies, waits for them, and re-layouts: 29.2 us -> 2.93 us  [the longest x2 2.22 us: to_slices(): pieces = jnp.swapaxes(block.reshape(rows, num_dp, width // num_dp), 0, 1)]
    all_to_all x0 -> x2, blocking collectives: none -> 17.4 us  [to_slices(): return lax.all_to_all(pieces, 'dp', split_axis=0, concat_axis=0, tiled=True)]
    all_gather x0 -> x2, waiting for transfers between devices: none -> 14.7 us  [the longest x1 14.7 us: shards(): lax.all_gather(to_slices(cotangent, num_dp), 'expert', axis=0, tiled=True)]
  transfers between devices with their start and end apart: 4 -> 7, of which waited for: 4 -> 5; matrix products, arithmetic and copies ran while one was open for 11% -> 13% of each run, Pallas kernels for 0% -> 0%
where the time goes in v1:
time: 276 us
  waiting for transfers between devices  104 us (38%)
  blocking collectives  85 us (31%)
  matrix products  60 us (22%)
  between operations  14 us (5%)
  starting transfers between devices  7.47 us (3%)
  local copies, waits for them, and re-layouts  3.42 us (1%)
    all_gather x1, blocking collectives, shards(): routing = lax.all_gather(routing, ('expert', 'dp'), axis=0, tiled=True)  67.5 us
    reduce_scatter x1, waiting for transfers between devices, shards(): lax.psum_scatter(tokens_back, 'expert', scatter_dimension=0, tiled=True)  52.5 us
    ppermute x3, waiting for transfers between devices, dp_total(): lax.ppermute(sent, 'dp', [(i, (i + shift) % num_dp) for i in range(num_dp)])  36.3 us
    dot_general x4, matrix products, contract_rows(): lax.dot_general(left, right, (((0,), (0,)), ((), ())), preferred_element_...  35.3 us
    all_to_all x2, blocking collectives, to_slices(): return lax.all_to_all(pieces, 'dp', split_axis=0, concat_axis=0, tiled=True)  17.4 us
    all_gather x1, waiting for transfers between devices, shards(): lax.all_gather(to_slices(cotangent, num_dp), 'expert', axis=0, tiled=True)  14.7 us
    dot_general x2, matrix products, contract_last(): lax.dot_general(left, right, (((1,), (1,)), ((), ())), preferred_element_...  11.3 us
  transfers between devices with their start and end apart: 7, of which 5 were waited for; matrix products, arithmetic and copies ran while one was open for 13% of the time, Pallas kernels for 0%

profile of v1, /device:TPU:0, one launch (start us, length us, event | category | flops | bytes accessed | tf_op | source)
XLA Modules:
  0.0 275.8 jit_solution(5199622743550688709)
XLA Ops:
  7.2 1.1 reshape.54
  8.4 9.4 %all_to_all.15 = bf16[2,16,3584]{2,1,0:T(8,128)(2,1)} all-to-all(bf16[2,16,3584]{2,1,0:T(8,128)(2,1)S(1)} %copy.28), channel_id=1, replica_groups=mesh['expert'=16,'dp'=2] {'dp'}, dimensions={0} | all-to-all | bytes 458752 | tf_op jit(solution)/shard_map/all_to_all | solution.py:31
  17.8 1.1 reshape.52
  19.0 8.1 %all_to_all.16 = bf16[2,16,3584]{2,1,0:T(8,128)(2,1)} all-to-all(bf16[2,16,3584]{2,1,0:T(8,128)(2,1)S(1)} %copy.27), channel_id=1, replica_groups=mesh['expert'=16,'dp'=2] {'dp'}, dimensions={0} | all-to-all | bytes 458752 | tf_op jit(solution)/shard_map/all_to_all | solution.py:31
  27.3 0.1 add.35
  27.4 67.5 %all_gather.9 = f32[512,16]{1,0:T(8,128)S(1)} all-gather(f32[16,16]{1,0:T(8,128)S(1)} %copy.26), channel_id=1, replica_groups=mesh['expert'=16,'dp'=2] {'expert','dp'}, dimensions={0}, use_global_device_ids=true | all-gather | bytes 33792 | tf_op jit(solution)/shard_map/all_gather | solution.py:70
  94.9 0.2 fusion.24
  95.2 0.1 reduce_or.9
  95.4 0.2 reduce_window_sum.13
  95.6 0.1 reduce_window_sum.14
  95.7 0.2 select_reduce_fusion
  95.9 4.8 %convolution_convert_fusion.4 = bf16[320,3584]{1,0:T(8,128)(2,1)} fusion(bf16[512,3584]{1,0:T(8,128)(2,1)} %bitcast.60, s32[512]{0:T(512)S(1)} %add_select_fusion), kind=kOutput, calls=%fused_computation.21 | convolution fusion | flops 1175715840 | bytes 5965824 | tf_op jit(solution)/shard_map/dot_general | solution.py:85
  100.7 14.7 %all-gather.3.cloned.1.call-done = bf16[32,16,3584]{2,1,0:T(8,128)(2,1)} async-done(((bf16[2,16,3584]{2,1,0:T(8,128)(2,1)}), bf16[32,16,3584]{2,1,0:T(8,128)(2,1)}) %all-gather.3.cloned.1.call-update) | async-done | bytes 3670032 | tf_op jit(solution)/shard_map/all_gather | solution.py:72
  115.4 3.5 %fusion.19 = bf16[320,3584]{1,0:T(8,128)(2,1)S(1)} fusion(bf16[512,3584]{1,0:T(8,128)(2,1)} %bitcast.61, f32[320]{0:T(512)S(1)} %select_reduce_fusion, s32[512]{0:T(512)S(1)} %add_select_fusion), kind=kOutput, calls=%fused_computation.20 | convolution fusion | flops 1176862720 | bytes 5967104 | tf_op jit(solution)/shard_map/dot_general | solution.py:88
  119.0 6.5 %fusion.30 = (bf16[320,1024]{1,0:T(8,128)(2,1)S(1)}, f32[320,1024]{1,0:T(8,128)S(1)}) fusion(bf16[320,3584]{1,0:T(8,128)(2,1)S(1)} %fusion.19, bf16[1,1024,3584]{2,1,0:T(8,128)(2,1)} %param.13), kind=kOutput, calls=%fused_computation.42 | convolution fusion | flops 2349137920 | bytes 11599872 | tf_op jit(solution)/shard_map/dot_general | solution.py:23
  125.6 1.5 collective-permute-start
  127.1 2.5 fusion.31
  129.7 0.6 collective-permute-start.2
  130.3 2.5 fusion.32
  132.8 1.5 collective-permute-start.1
  134.4 8.8 %collective-permute-done = bf16[320,1024]{1,0:T(8,128)(2,1)S(1)} collective-permute-done((bf16[320,1024]{1,0:T(8,128)(2,1)S(1)}, bf16[320,1024]{1,0:T(8,128)(2,1)S(1)}, u32[]{:S(2)}, u32[]{:S(2)}) %collective-permute-start) | collective-permute-done | bytes 655392 | tf_op jit(solution)/shard_map/ppermute | solution.py:38
  143.2 14.0 %collective-permute-done.2 = bf16[320,1024]{1,0:T(8,128)(2,1)S(1)} collective-permute-done((bf16[320,1024]{1,0:T(8,128)(2,1)S(1)}, bf16[320,1024]{1,0:T(8,128)(2,1)S(1)}, u32[]{:S(2)}, u32[]{:S(2)}) %collective-permute-start.2) | collective-permute-done | bytes 655392 | tf_op jit(solution)/shard_map/ppermute | solution.py:38
  157.3 13.4 %collective-permute-done.1 = bf16[320,1024]{1,0:T(8,128)(2,1)S(1)} collective-permute-done((bf16[320,1024]{1,0:T(8,128)(2,1)S(1)}, bf16[320,1024]{1,0:T(8,128)(2,1)S(1)}, u32[]{:S(2)}, u32[]{:S(2)}) %collective-permute-start.1) | collective-permute-done | bytes 655392 | tf_op jit(solution)/shard_map/ppermute | solution.py:38
  170.6 1.7 multiply_convert_fusion.1
  172.4 4.7 %fusion = f32[320,3584]{1,0:T(8,128)} fusion(bf16[320,1024]{1,0:T(8,128)(2,1)S(1)} %get-tuple-element.7, bf16[1,3584,1024]{2,1,0:T(8,128)(2,1)S(1)} %bitcast.57), kind=kOutput, calls=%fused_computation.3 | convolution fusion | flops 2348810240 | bytes 12582912 | tf_op jit(solution)/shard_map/dot_general | solution.py:23
  177.1 11.1 %convolution_convert_fusion.3 = bf16[512,3584]{1,0:T(8,128)(2,1)} fusion(s32[512]{0:T(512)S(1)} %add_select_fusion, f32[320,3584]{1,0:T(8,128)} %fusion, bf16[320,1024]{1,0:T(8,128)(2,1)} %get-tuple-element.6, bf16[1,3584,1024]{2,1,0:T(8,128)(2,1)} %param.12), kind=kOutput, calls=%fused_computation.16 | convolution fusion | flops 3527507968 | bytes 16254976 | tf_op jit(solution)/shard_map/dot_general | solution.py:17
  188.2 9.0 %fusion.11 = bf16[1,3584,1024]{2,1,0:T(8,128)(2,1)} fusion(bf16[320,3584]{1,0:T(8,128)(2,1)} %convolution_convert_fusion.4, bf16[320,1024]{1,0:T(8,128)(2,1)} %get-tuple-element.6), kind=kOutput, calls=%fused_computation.14 | convolution fusion | flops 2352480256 | bytes 10289152 | tf_op jit(solution)/shard_map/dot_general | solution.py:17
  197.2 6.3 %fusion.12 = bf16[1,1024,3584]{2,1,0:T(8,128)(2,1)} fusion(bf16[320,3584]{1,0:T(8,128)(2,1)S(1)} %copy-done.7, f32[320,1024]{1,0:T(8,128)S(1)} %get-tuple-element.13, bf16[320,1024]{1,0:T(8,128)(2,1)S(1)} %copy-done.1, f32[320,1024]{1,0:T(8,128)S(1)} %get-tuple-element.11, bf16[320,1024]{1,0:T(8,128)(2,1)S(1)} %collective-permute-done.2), kind=kOutput, calls=%fused_computation.15 | convolution fusion | flops 2355757056 | bytes 13565952 | tf_op jit(solution)/shard_map/dot_general | solution.py:17
  203.6 52.5 %reduce-scatter.2.cloned.1.call-done = bf16[32,3584]{1,0:T(8,128)(2,1)} async-done(((bf16[512,3584]{1,0:T(8,128)(2,1)}), bf16[32,3584]{1,0:T(8,128)(2,1)}) %reduce-scatter.2.cloned.1.call-update) | async-done | bytes 229392 | tf_op jit(solution)/shard_map/reduce_scatter | solution.py:95
  256.1 3.7 %all-to-all-start.2 = ((bf16[2,16,3584]{2,1,0:T(8,128)(2,1)}), bf16[2,16,3584]{2,1,0:T(8,128)(2,1)S(1)}, u32[]{:S(2)}, u32[]{:S(2)}) async-start(bf16[2,16,3584]{2,1,0:T(8,128)(2,1)} %bitcast.54), calls=%async_computation.3 | async-start | bytes 458752 | tf_op jit(solution)/shard_map/all_to_all | solution.py:100
  259.8 8.8 %fusion.10 = bf16[1,3584,1024]{2,1,0:T(8,128)(2,1)} fusion(bf16[320,3584]{1,0:T(8,128)(2,1)} %convolution_convert_fusion.4, bf16[320,1024]{1,0:T(8,128)(2,1)} %copy-done.2), kind=kOutput, calls=%fused_computation.13 | convolution fusion | flops 2352480256 | bytes 10289152 | tf_op jit(solution)/shard_map/dot_general | solution.py:17
  268.6 0.7 copy.30
  (44 shorter events, 0.6 us)
Async XLA Ops:
  7.2 19.9 %copy-start.3 = (s32[16,8]{0,1:T(8,128)S(1)}, s32[16,8]{0,1:T(8,128)}, u32[]{:S(2)}) copy-start(s32[16,8]{0,1:T(8,128)} %param.9) | copy-start | bytes 1540
  7.2 20.0 %copy-start.4 = (f32[16,8]{0,1:T(8,128)S(1)}, f32[16,8]{0,1:T(8,128)}, u32[]{:S(2)}) copy-start(f32[16,8]{0,1:T(8,128)} %param.10) | copy-start | bytes 1540
  7.2 88.7 %all-gather.5.cloned.1.call-start = ((), (), s32[]{:S(2)}) async-start(), calls=%async_computation.5 | async-start | bytes 3899392 | tf_op jit(solution)/shard_map/all_gather | solution.py:71
  17.8 97.7 %all-gather.3.cloned.1.call-start = ((), (), s32[]{:S(2)}) async-start(), calls=%async_computation.4 | async-start | bytes 3899392 | tf_op jit(solution)/shard_map/all_gather | solution.py:72
  27.1 229.0 %reduce-scatter.2.cloned.1.call-start = ((), (), s32[]{:S(2)}) async-start(), calls=%async_computation.6 | async-start | bytes 3899392 | tf_op jit(solution)/shard_map/reduce_scatter | solution.py:95
  115.4 11.7 %slice-start = ((s8[7340032]{0:T(1024)(128)(4,1)}), s8[4194304]{0:T(1024)(128)(4,1)S(1)}, s32[]{:S(2)}) async-start(s8[7340032]{0:T(1024)(128)(4,1)} %bitcast.56), calls=%async_computation.7 | async-start | bytes 8388608
  119.0 6.6 %copy-start.6 = (bf16[320,3584]{1,0:T(8,128)(2,1)}, bf16[320,3584]{1,0:T(8,128)(2,1)S(1)}, u32[]{:S(2)}) copy-start(bf16[320,3584]{1,0:T(8,128)(2,1)S(1)} %fusion.19) | copy-start | bytes 6881284
  119.0 8.1 %slice-start.1 = ((s8[7340032]{0:T(1024)(128)(4,1)}), s8[3145728]{0:T(1024)(128)(4,1)S(1)}, s32[]{:S(2)}) async-start(s8[7340032]{0:T(1024)(128)(4,1)} %bitcast.56), calls=%async_computation.8 | async-start | bytes 6291456
  119.0 8.1 %copy-start.5 = (bf16[320,3584]{1,0:T(8,128)(2,1)S(1)}, bf16[320,3584]{1,0:T(8,128)(2,1)}, u32[]{:S(2)}) copy-start(bf16[320,3584]{1,0:T(8,128)(2,1)} %convolution_convert_fusion.4) | copy-start | bytes 6881284
  125.6 4.7 %slice-start.2 = ((s8[7340032]{0:T(1024)(128)(4,1)}), s8[4194304]{0:T(1024)(128)(4,1)S(1)}, s32[]{:S(2)}) async-start(s8[7340032]{0:T(1024)(128)(4,1)} %bitcast.58), calls=%async_computation.9 | async-start | bytes 8388608
  125.6 4.7 %slice-start.3 = ((s8[7340032]{0:T(1024)(128)(4,1)}), s8[3145728]{0:T(1024)(128)(4,1)S(1)}, s32[]{:S(2)}) async-start(s8[7340032]{0:T(1024)(128)(4,1)} %bitcast.58), calls=%async_computation.10 | async-start | bytes 6291456
  125.6 17.6 %collective-permute-start = (bf16[320,1024]{1,0:T(8,128)(2,1)S(1)}, bf16[320,1024]{1,0:T(8,128)(2,1)S(1)}, u32[]{:S(2)}, u32[]{:S(2)}) collective-permute-start(bf16[320,1024]{1,0:T(8,128)(2,1)S(1)} %get-tuple-element.8), channel_id=1, source_target_pairs={{0,1},{1,0},{2,3},{3,2},{4,5},{5,4},{6,7},{7,6},{8,9},{9,8},{10,11... | collective-permute-start | bytes 1966088 | tf_op jit(solution)/shard_map/ppermute | solution.py:38
  129.7 27.6 %collective-permute-start.2 = (bf16[320,1024]{1,0:T(8,128)(2,1)S(1)}, bf16[320,1024]{1,0:T(8,128)(2,1)S(1)}, u32[]{:S(2)}, u32[]{:S(2)}) collective-permute-start(bf16[320,1024]{1,0:T(8,128)(2,1)S(1)} %get-tuple-element.10), channel_id=1, source_target_pairs={{0,1},{1,0},{2,3},{3,2},{4,5},{5,4},{6,7},{7,6},{8,9},{9,8},{10,11... | collective-permute-start | bytes 1966088 | tf_op jit(solution)/shard_map/ppermute | solution.py:38
  132.8 37.8 %collective-permute-start.1 = (bf16[320,1024]{1,0:T(8,128)(2,1)S(1)}, bf16[320,1024]{1,0:T(8,128)(2,1)S(1)}, u32[]{:S(2)}, u32[]{:S(2)}) collective-permute-start(bf16[320,1024]{1,0:T(8,128)(2,1)S(1)} %get-tuple-element.12), channel_id=1, source_target_pairs={{0,1},{1,0},{2,3},{3,2},{4,5},{5,4},{6,7},{7,6},{8,9},{9,8},{10,11... | collective-permute-start | bytes 1966088 | tf_op jit(solution)/shard_map/ppermute | solution.py:38
  170.6 1.7 copy-start
  172.4 4.7 %copy-start.2 = (bf16[320,1024]{1,0:T(8,128)(2,1)}, bf16[320,1024]{1,0:T(8,128)(2,1)S(1)}, u32[]{:S(2)}) copy-start(bf16[320,1024]{1,0:T(8,128)(2,1)S(1)} %get-tuple-element.7) | copy-start | bytes 1966084
  188.2 9.0 %copy-start.1 = (bf16[320,1024]{1,0:T(8,128)(2,1)S(1)}, bf16[320,1024]{1,0:T(8,128)(2,1)}, u32[]{:S(2)}) copy-start(bf16[320,1024]{1,0:T(8,128)(2,1)} %copy-done) | copy-start | bytes 1966084
  188.2 9.0 %copy-start.7 = (bf16[320,3584]{1,0:T(8,128)(2,1)S(1)}, bf16[320,3584]{1,0:T(8,128)(2,1)}, u32[]{:S(2)}) copy-start(bf16[320,3584]{1,0:T(8,128)(2,1)} %copy-done.6) | copy-start | bytes 6881284
  256.1 12.5 %all-to-all-start.2 = ((bf16[2,16,3584]{2,1,0:T(8,128)(2,1)}), bf16[2,16,3584]{2,1,0:T(8,128)(2,1)S(1)}, u32[]{:S(2)}, u32[]{:S(2)}) async-start(bf16[2,16,3584]{2,1,0:T(8,128)(2,1)} %bitcast.54), calls=%async_computation.3 | async-start | bytes 458752 | tf_op jit(solution)/shard_map/all_to_all | solution.py:100
Sparse Core Ops, SparseCore 0:
  17.9 48.5 all-gather.4
  68.8 46.6 all-gather.2
  188.3 67.7 reduce-scatter.1

commit v2 on v1

--- a/solution.py
+++ b/solution.py
@@ -1,6 +1,9 @@
+import functools
 import jax
 import jax.numpy as jnp
 from jax import lax
+from jax.experimental import pallas as pl
+from jax.experimental.pallas import tpu as pltpu
 from jax.sharding import PartitionSpec as P
 
 
@@ -25,10 +28,193 @@
     )
 
 
-def to_slices(block, num_dp):
-    rows, width = block.shape
-    pieces = jnp.swapaxes(block.reshape(rows, num_dp, width // num_dp), 0, 1)
-    return lax.all_to_all(pieces, "dp", split_axis=0, concat_axis=0, tiled=True)
+MESH = pl.DeviceIdType.MESH
+LANES = 128
+CORES = 2
+OUTER = 4
+
+
+def gather_kernel(
+    num_exp, num_dp, sent, out, own_sem, x_send, x_recv, r_send, r_recv,
+    m_send, m_recv, c_send, c_recv,
+):
+    middle = num_exp // (OUTER * CORES)
+    e = lax.axis_index("expert")
+    d = lax.axis_index("dp")
+    core = lax.rem(e, CORES)
+    mid = lax.rem(e // CORES, middle)
+    outer = e // (CORES * middle)
+
+    def at(o, m, c):
+        return (lax.rem(o + OUTER, OUTER) * middle + lax.rem(m + middle, middle)) * CORES + c
+
+    def copy(src, dst, send, recv, device):
+        return pltpu.make_async_remote_copy(
+            src_ref=src, dst_ref=dst, send_sem=send, recv_sem=recv,
+            device_id=device, device_id_type=MESH,
+        )
+
+    barrier = pltpu.get_barrier_semaphore()
+    partners = [(e, lax.rem(d + k, num_dp)) for k in range(1, num_dp)]
+    partners += [(at(outer + 1, mid, core), d), (at(outer - 1, mid, core), d)]
+    partners += [(at(outer, mid + k, core), d) for k in range(1, middle)]
+    partners += [(at(outer, mid, 1 - core), d)]
+    for partner in partners:
+        pl.semaphore_signal(barrier, inc=1, device_id=partner, device_id_type=MESH)
+    pl.semaphore_wait(barrier, len(partners))
+
+    started = []
+    for k in range(1, num_dp):
+        to = lax.rem(d + k, num_dp)
+        c = copy(sent.at[to], out.at[e, d], x_send.at[k], x_recv.at[k], (e, to))
+        c.start()
+        started.append(c)
+    own = pltpu.make_async_copy(sent.at[d], out.at[e, d], own_sem)
+    own.start()
+    own.wait()
+    for k in range(1, num_dp):
+        came = lax.rem(d - k + num_dp, num_dp)
+        copy(sent.at[d], out.at[e, came], x_send.at[k], x_recv.at[k], (e, came)).wait_recv()
+
+    def to_core(unit, k, s):
+        c = copy(
+            out.at[unit], out.at[unit], c_send.at[k, s], c_recv.at[k, s],
+            (at(outer, mid, 1 - core), d),
+        )
+        c.start()
+        started.append(c)
+
+    def forward_middle(s):
+        for k in range(1, middle):
+            unit = at(outer - s, mid - k, core)
+            copy(
+                out.at[unit], out.at[unit], m_send.at[k, s], m_recv.at[k, s],
+                (at(outer, mid - k, core), d),
+            ).wait_recv()
+            to_core(unit, k, s)
+
+    for s in range(OUTER):
+        unit = at(outer - s, mid, core)
+        if s > 0:
+            copy(
+                out.at[unit], out.at[unit], r_send.at[s - 1], r_recv.at[s - 1],
+                (at(outer - 1, mid, core), d),
+            ).wait_recv()
+        if s < OUTER - 1:
+            c = copy(
+                out.at[unit], out.at[unit], r_send.at[s], r_recv.at[s],
+                (at(outer + 1, mid, core), d),
+            )
+            c.start()
+            started.append(c)
+        for k in range(1, middle):
+            c = copy(
+                out.at[unit], out.at[unit], m_send.at[k, s], m_recv.at[k, s],
+                (at(outer, mid + k, core), d),
+            )
+            c.start()
+            started.append(c)
+        to_core(unit, 0, s)
+        if s > 0:
+            forward_middle(s - 1)
+    forward_middle(OUTER - 1)
+    for s in range(OUTER):
+        for k in range(middle):
+            unit = at(outer - s, mid - k, 1 - core)
+            copy(
+                out.at[unit], out.at[unit], c_send.at[k, s], c_recv.at[k, s],
+                (at(outer, mid, 1 - core), d),
+            ).wait_recv()
+    for c in started:
+        c.wait_send()
+
+
+def gather_units(sent, num_exp, num_dp):
+    middle = num_exp // (OUTER * CORES)
+    dma = pltpu.SemaphoreType.DMA
+    return pl.pallas_call(
+        functools.partial(gather_kernel, num_exp, num_dp),
+        out_shape=jax.ShapeDtypeStruct((num_exp,) + sent.shape, sent.dtype),
+        in_specs=[pl.BlockSpec(memory_space=pl.ANY)],
+        out_specs=pl.BlockSpec(memory_space=pl.ANY),
+        scratch_shapes=[
+            dma(()),
+            dma((num_dp,)),
+            dma((num_dp,)),
+            dma((OUTER,)),
+            dma((OUTER,)),
+            dma((middle, OUTER)),
+            dma((middle, OUTER)),
+            dma((middle, OUTER)),
+            dma((middle, OUTER)),
+        ],
+        compiler_params=pltpu.CompilerParams(collective_id=0, has_side_effects=True),
+    )(sent)
+
+
+def units_to_send(activations, cotangent, route_ids, route_weights, num_dp):
+    rows, width = activations.shape
+    topk = route_ids.shape[1]
+    high = lax.reduce_precision(route_weights, 8, 7)
+    rest = route_weights - high
+    middle = lax.reduce_precision(rest, 8, 7)
+    low = rest - middle
+    routing = jnp.concatenate([route_ids.astype(jnp.float32), high, middle, low], axis=1)
+    routing = jnp.pad(routing, ((0, 0), (0, LANES - 4 * topk))).astype(jnp.bfloat16)
+    routing = jnp.broadcast_to(routing[None, None], (num_dp, 2, rows, LANES))
+    both = jnp.stack([activations, cotangent]).reshape(2, rows, num_dp, width // num_dp)
+    both = jnp.transpose(both, (2, 0, 1, 3))
+    return jnp.concatenate([both, routing], axis=3)
+
+
+def to_owners(back, num_exp, num_dp, tok_rows):
+    middle = num_exp // (OUTER * CORES)
+    e = lax.axis_index("expert")
+    d = lax.axis_index("dp")
+    core = lax.rem(e, CORES)
+    mid = lax.rem(e // CORES, middle)
+    outer = e // (CORES * middle)
+    cols = back.shape[1]
+
+    def shifted(o, m, c):
+        return [
+            (
+                i,
+                ((i // (CORES * middle) + o) % OUTER * middle + (i // CORES + m) % middle) * CORES
+                + (i + c) % CORES,
+            )
+            for i in range(num_exp)
+        ]
+
+    def pick(array, index, axis):
+        return lax.dynamic_index_in_dim(array, index, axis, keepdims=False)
+
+    units = back.reshape(OUTER, middle, CORES, num_dp * tok_rows, cols)
+    total = pick(units, core, 2).astype(jnp.float32)
+    got = lax.ppermute(pick(units, 1 - core, 2), "expert", shifted(0, 0, 1))
+    units = (total + got.astype(jnp.float32)).astype(jnp.bfloat16)
+    total = pick(units, mid, 1).astype(jnp.float32)
+    for k in range(1, middle):
+        got = lax.ppermute(
+            pick(units, lax.rem(mid + k, middle), 1), "expert", shifted(0, k, 0)
+        )
+        total = total + got.astype(jnp.float32)
+    units = total.astype(jnp.bfloat16)
+    total = pick(units, outer, 0).astype(jnp.float32)
+    for k in range(1, OUTER):
+        got = lax.ppermute(pick(units, lax.rem(outer + k, OUTER), 0), "expert", shifted(k, 0, 0))
+        total = total + got.astype(jnp.float32)
+    total = total.astype(jnp.bfloat16).reshape(num_dp, tok_rows, cols)
+    pieces = jnp.zeros_like(total)
+    pieces = lax.dynamic_update_index_in_dim(pieces, pick(total, d, 0), d, 0)
+    for k in range(1, num_dp):
+        got = lax.ppermute(
+            pick(total, lax.rem(d + k, num_dp), 0),
+            "dp",
+            [(i, (i + k) % num_dp) for i in range(num_dp)],
+        )
+        pieces = lax.dynamic_update_index_in_dim(pieces, got, lax.rem(d - k + num_dp, num_dp), 0)
+    return pieces
 
 
 def dp_total(part, num_dp):
@@ -66,15 +252,15 @@
     slice_width = gate_weights.shape[1]
     tokens = tok_rows * num_exp * num_dp
     capacity = min(tok_rows, 5 * tok_rows * topk // (4 * num_exp))
-    routing = jnp.concatenate([route_ids.astype(jnp.float32), route_weights], axis=1)
-    routing = lax.all_gather(routing, ("expert", "dp"), axis=0, tiled=True)
-    all_act = lax.all_gather(to_slices(activations, num_dp), "expert", axis=0, tiled=True)
-    all_cot = lax.all_gather(to_slices(cotangent, num_dp), "expert", axis=0, tiled=True)
-    all_act = all_act.reshape(tokens, slice_width)
-    all_cot = all_cot.reshape(tokens, slice_width)
+    sent = units_to_send(activations, cotangent, route_ids, route_weights, num_dp)
+    units = gather_units(sent, num_exp, num_dp)
+    all_act = units[:, :, 0, :, :slice_width].reshape(tokens, slice_width)
+    all_cot = units[:, :, 1, :, :slice_width].reshape(tokens, slice_width)
+    routing = units[:, :, 0, :, slice_width:].astype(jnp.float32).reshape(tokens, LANES)
+    weights = routing[:, topk : 2 * topk] + routing[:, 2 * topk : 3 * topk]
     placing, row_weight = placement(
         routing[:, :topk].astype(jnp.int32),
-        routing[:, topk:],
+        weights + routing[:, 3 * topk : 4 * topk],
         capacity,
         tok_rows,
         lax.axis_index("expert"),
@@ -89,15 +275,17 @@
     cot_rows = (cot_rows * row_weight[:, None]).astype(jnp.bfloat16)
     upstream = dp_total(contract_last(cot_rows, down_local), num_dp)
     grad_pre, grad_lin, activated = swiglu_back(gate, upper, upstream)
-    rows_back = contract_last(grad_pre, gate_local) + contract_last(grad_lin, up_local)
-    rows_back = rows_back.astype(jnp.bfloat16)
-    tokens_back = contract_rows(placing, rows_back).astype(jnp.bfloat16)
-    arrived = lax.psum_scatter(tokens_back, "expert", scatter_dimension=0, tiled=True)
+    halves = []
+    half = slice_width // 2
+    for start in (0, half):
+        rows_back = contract_last(grad_pre, gate_local[start : start + half])
+        rows_back = rows_back + contract_last(grad_lin, up_local[start : start + half])
+        back = contract_rows(placing, rows_back.astype(jnp.bfloat16)).astype(jnp.bfloat16)
+        halves.append(to_owners(back, num_exp, num_dp, tok_rows))
     grad_gate = contract_rows(act_rows, grad_pre).astype(jnp.bfloat16)[None]
     grad_up = contract_rows(act_rows, grad_lin).astype(jnp.bfloat16)[None]
     grad_down = contract_rows(activated, cot_rows).astype(jnp.bfloat16)[None]
-    arrived = arrived.reshape(num_dp, tok_rows, slice_width)
-    arrived = lax.all_to_all(arrived, "dp", split_axis=0, concat_axis=0, tiled=True)
+    arrived = jnp.concatenate(halves, axis=2)
     grad_input = jnp.swapaxes(arrived, 0, 1).reshape(tok_rows, width)
     return (grad_input, grad_gate, grad_up, grad_down)
 

time: 276 us -> 223 us (0.81)
  blocking collectives: 85 us -> 0 us
  Pallas kernels: 0 us -> 60.2 us
  waiting for transfers between devices: 104 us -> 58.1 us
  between operations: 14 us -> 1.04 us
  local copies, waits for them, and re-layouts: 3.42 us -> 14.8 us
  starting transfers between devices: 7.47 us -> 18.7 us
  other arithmetic: 2.48 us -> 8.91 us
    all_gather x1 -> x0, blocking collectives: 67.5 us -> none  [shards(): routing = lax.all_gather(routing, ('expert', 'dp'), axis=0, tiled=True)]
    pallas_call x0 -> x1, Pallas kernels: none -> 60.2 us  [gather_units(): pl.pallas_call(functools.partial(gather_kernel, num_exp, num_dp), out_sha...]
    reduce_scatter x1 -> x0, waiting for transfers between devices: 52.5 us -> none  [shards(): lax.psum_scatter(tokens_back, 'expert', scatter_dimension=0, tiled=True)]
    ppermute x0 -> x12, waiting for transfers between devices: none -> 24.4 us  [the longest x2 15.1 us: to_owners(): lax.ppermute(pick(units, lax.rem(mid + k, middle), 1), 'expert', shifted(...]
    all_to_all x2 -> x0, blocking collectives: 17.4 us -> none  [to_slices(): return lax.all_to_all(pieces, 'dp', split_axis=0, concat_axis=0, tiled=True)]
    ppermute x0 -> x12, starting transfers between devices: none -> 15.2 us  [the longest x6 9.05 us: to_owners(): lax.ppermute(pick(units, lax.rem(outer + k, OUTER), 0), 'expert', shifted...]
    all_gather x2 -> x0, waiting for transfers between devices: 14.7 us -> none  [the longest x1 14.7 us: shards(): lax.all_gather(to_slices(cotangent, num_dp), 'expert', axis=0, tiled=True)]
    slice x0 -> x2, local copies, waits for them, and re-layouts: none -> 7.91 us  [the longest x1 6.99 us: shards(): all_act = units[:, :, 0, :, :slice_width].reshape(tokens, slice_width)]
  transfers between devices with their start and end apart: 7 -> 15, of which waited for: 5 -> 9; matrix products, arithmetic and copies ran while one was open for 13% -> 17% of each run, Pallas kernels for 0% -> 0%
where the time goes in v2:
time: 223 us
  matrix products  60.8 us (27%)
  Pallas kernels  60.2 us (27%)
  waiting for transfers between devices  58.1 us (26%)
  starting transfers between devices  18.7 us (8%)
  local copies, waits for them, and re-layouts  14.8 us (7%)
  other arithmetic  8.91 us (4%)
    pallas_call x1, Pallas kernels, gather_units(): pl.pallas_call(functools.partial(gather_kernel, num_exp, num_dp), out_sha...  60.2 us
    ppermute x3, waiting for transfers between devices, dp_total(): lax.ppermute(sent, 'dp', [(i, (i + shift) % num_dp) for i in range(num_dp)])  33.7 us
    dot_general x5, matrix products, contract_rows(): lax.dot_general(left, right, (((0,), (0,)), ((), ())), preferred_element_...  33.3 us
    dot_general x3, matrix products, contract_last(): lax.dot_general(left, right, (((1,), (1,)), ((), ())), preferred_element_...  15.9 us
    ppermute x2, waiting for transfers between devices, to_owners(): lax.ppermute(pick(units, lax.rem(mid + k, middle), 1), 'expert', shifted(...  15.1 us
    ppermute x6, starting transfers between devices, to_owners(): lax.ppermute(pick(units, lax.rem(outer + k, OUTER), 0), 'expert', shifted...  9.05 us
    slice x1, local copies, waits for them, and re-layouts, shards(): all_act = units[:, :, 0, :, :slice_width].reshape(tokens, slice_width)  6.99 us
    ppermute x6, waiting for transfers between devices, to_owners(): lax.ppermute(pick(units, lax.rem(outer + k, OUTER), 0), 'expert', shifted...  6.85 us
  transfers between devices with their start and end apart: 15, of which 9 were waited for; matrix products, arithmetic and copies ran while one was open for 17% of the time, Pallas kernels for 0%

profile of v2, /device:TPU:0, one launch (start us, length us, event | category | flops | bytes accessed | tf_op | source)
XLA Modules:
  0.0 222.5 jit_solution(9775939135877140949)
XLA Ops:
  5.3 60.2 %shard_map.102 = bf16[16,2,2,16,3712]{4,3,2,1,0:T(8,128)(2,1)} custom-call(bf16[2,2,16,3712]{3,2,1,0:T(8,128)(2,1)} %pad_maximum_fusion.sent), custom_call_target="tpu_custom_call" | custom-call | tf_op jit(solution)/shard_map/pallas_call | solution.py:135
  66.4 7.0 %fusion.60 = (bf16[16,2,1,16,3584]{4,3,2,1,0:T(8,128)(2,1)}, bf16[16,2,1,16,3584]{4,3,2,1,0:T(8,128)(2,1)}) fusion(bf16[16,2,2,16,3712]{4,3,2,1,0:T(8,128)(2,1)} %shard_map.102), kind=kLoop, calls=%fused_computation.97 | loop fusion | bytes 14680064 | tf_op jit(solution)/shard_map/slice | solution.py:257
  74.7 3.5 %fusion.9 = bf16[320,3584]{1,0:T(8,128)(2,1)S(1)} fusion(bf16[512,3584]{1,0:T(8,128)(2,1)} %bitcast.118, f32[320]{0:T(512)S(1)} %select_reduce_fusion, s32[512]{0:T(512)S(1)} %add_select_fusion), kind=kOutput, calls=%fused_computation.13 | convolution fusion | flops 1176862720 | bytes 5967104 | tf_op jit(solution)/shard_map/dot_general | solution.py:274
  78.3 7.8 %fusion.61 = (bf16[320,1024]{1,0:T(8,128)(2,1)}, f32[320,1024]{1,0:T(8,128)}) fusion(bf16[320,3584]{1,0:T(8,128)(2,1)S(1)} %fusion.9, bf16[1,1024,3584]{2,1,0:T(8,128)(2,1)} %param.13), kind=kOutput, calls=%fused_computation.98 | convolution fusion | flops 2349137920 | bytes 11599872 | tf_op jit(solution)/shard_map/dot_general | solution.py:26
  86.1 1.5 collective-permute-start
  89.0 3.4 %fusion.62 = (bf16[320,1024]{1,0:T(8,128)(2,1)}, f32[320,1024]{1,0:T(8,128)S(1)}) fusion(bf16[320,3584]{1,0:T(8,128)(2,1)S(1)} %convolution_convert_fusion.3, bf16[1,3584,1024]{2,1,0:T(8,128)(2,1)S(1)} %bitcast.130), kind=kOutput, calls=%fused_computation.99 | convolution fusion | flops 2349137920 | bytes 11599872 | tf_op jit(solution)/shard_map/dot_general | solution.py:272
  92.9 3.4 %fusion.63 = (bf16[320,1024]{1,0:T(8,128)(2,1)}, f32[320,1024]{1,0:T(8,128)S(1)}) fusion(bf16[320,3584]{1,0:T(8,128)(2,1)S(1)} %convolution_convert_fusion.3, bf16[1,3584,1024]{2,1,0:T(8,128)(2,1)S(1)} %bitcast.134), kind=kOutput, calls=%fused_computation.100 | convolution fusion | flops 2349137920 | bytes 11599872 | tf_op jit(solution)/shard_map/dot_general | solution.py:273
  96.3 1.5 collective-permute-start.1
  97.8 6.1 %collective-permute-done = bf16[320,1024]{1,0:T(8,128)(2,1)} collective-permute-done((bf16[320,1024]{1,0:T(8,128)(2,1)}, bf16[320,1024]{1,0:T(8,128)(2,1)}, u32[]{:S(2)}, u32[]{:S(2)}) %collective-permute-start) | collective-permute-done | bytes 655392 | tf_op jit(solution)/shard_map/ppermute | solution.py:224
  103.9 13.9 %collective-permute-done.2 = bf16[320,1024]{1,0:T(8,128)(2,1)S(1)} collective-permute-done((bf16[320,1024]{1,0:T(8,128)(2,1)}, bf16[320,1024]{1,0:T(8,128)(2,1)S(1)}, u32[]{:S(2)}, u32[]{:S(2)}) %collective-permute-start.2) | collective-permute-done | bytes 655392 | tf_op jit(solution)/shard_map/ppermute | solution.py:224
  117.9 13.7 %collective-permute-done.1 = bf16[320,1024]{1,0:T(8,128)(2,1)} collective-permute-done((bf16[320,1024]{1,0:T(8,128)(2,1)}, bf16[320,1024]{1,0:T(8,128)(2,1)}, u32[]{:S(2)}, u32[]{:S(2)}) %collective-permute-start.1) | collective-permute-done | bytes 655392 | tf_op jit(solution)/shard_map/ppermute | solution.py:224
  131.5 3.6 %multiply_convert_fusion.1 = (bf16[320,1024]{1,0:T(8,128)(2,1)}, bf16[320,1024]{1,0:T(8,128)(2,1)S(1)}) fusion(f32[320,1024]{1,0:T(8,128)} %get-tuple-element.24, bf16[320,1024]{1,0:T(8,128)(2,1)} %collective-permute-done, f32[320,1024]{1,0:T(8,128)S(1)} %get-tuple-element.26, bf16[320,1024]{1,0:T(8,128)(2,1)S(1)} %collective-permute-done.2, ...), kind=kLoop, calls=%fused_computation.38 | loop fusion | flops 6225920 | bytes 7208960 | tf_op jit(solution)/shard_map/convert_element_type | solution.py:15
  135.1 5.1 %fusion.12 = f32[320,1792]{1,0:T(8,128)} fusion(bf16[320,1024]{1,0:T(8,128)(2,1)S(1)} %get-tuple-element.9, bf16[1,3584,1024]{2,1,0:T(8,128)(2,1)} %param.11), kind=kOutput, calls=%fused_computation.17 | convolution fusion | flops 1174405120 | bytes 6619136 | tf_op jit(solution)/shard_map/dot_general | solution.py:26
  140.2 3.0 %fusion.16 = f32[320,1792]{1,0:T(8,128)} fusion(bf16[320,1024]{1,0:T(8,128)(2,1)S(1)} %get-tuple-element.9, bf16[1,3584,1024]{2,1,0:T(8,128)(2,1)S(1)} %bitcast.132), kind=kOutput, calls=%fused_computation.21 | convolution fusion | flops 1174405120 | bytes 6619136 | tf_op jit(solution)/shard_map/dot_general | solution.py:26
  143.2 5.4 %convolution_convert_fusion.4 = bf16[512,1792]{1,0:T(8,128)(2,1)S(1)} fusion(f32[320,1792]{1,0:T(8,128)} %fusion.12, bf16[320,1024]{1,0:T(8,128)(2,1)} %get-tuple-element.8, bf16[1,3584,1024]{2,1,0:T(8,128)(2,1)} %param.12, s32[512]{0:T(512)S(1)} %add_select_fusion), kind=kOutput, calls=%fused_computation.27 | convolution fusion | flops 1763835904 | bytes 8456192 | tf_op jit(solution)/shard_map/dot_general | solution.py:20
  150.2 5.4 %convolution_convert_fusion.5 = bf16[512,1792]{1,0:T(8,128)(2,1)S(1)} fusion(f32[320,1792]{1,0:T(8,128)} %fusion.16, bf16[320,1024]{1,0:T(8,128)(2,1)} %get-tuple-element.8, bf16[1,3584,1024]{2,1,0:T(8,128)(2,1)} %param.12, s32[512]{0:T(512)S(1)} %add_select_fusion), kind=kOutput, calls=%fused_computation.28 | convolution fusion | flops 1763835904 | bytes 8456192 | tf_op jit(solution)/shard_map/dot_general | solution.py:20
  156.3 10.0 %fusion.8 = bf16[1,1024,3584]{2,1,0:T(8,128)(2,1)} fusion(bf16[320,3584]{1,0:T(8,128)(2,1)} %copy-done.10, f32[320,1024]{1,0:T(8,128)} %copy-done.3, bf16[320,1024]{1,0:T(8,128)(2,1)} %collective-permute-done.1, f32[320,1024]{1,0:T(8,128)S(1)} %get-tuple-element.26, bf16[320,1024]{1,0:T(8,128)(2,1)} %copy-done.4), kind=kOutput, calls=%fused_computation.11 | convolution fusion | flops 2355757056 | bytes 13565952 | tf_op jit(solution)/shard_map/dot_general | solution.py:20
  166.3 6.3 %fusion.7 = bf16[1,3584,1024]{2,1,0:T(8,128)(2,1)} fusion(bf16[320,3584]{1,0:T(8,128)(2,1)S(1)} %copy-done.9, bf16[320,1024]{1,0:T(8,128)(2,1)S(1)} %copy-done.7), kind=kOutput, calls=%fused_computation.10 | convolution fusion | flops 2352480256 | bytes 10289152 | tf_op jit(solution)/shard_map/dot_general | solution.py:20
  172.6 6.1 %fusion.6 = bf16[1,3584,1024]{2,1,0:T(8,128)(2,1)} fusion(bf16[320,3584]{1,0:T(8,128)(2,1)S(1)} %copy-done.9, bf16[320,1024]{1,0:T(8,128)(2,1)S(1)} %copy-done.6), kind=kOutput, calls=%fused_computation.9 | convolution fusion | flops 2352480256 | bytes 10289152 | tf_op jit(solution)/shard_map/dot_general | solution.py:20
  178.7 1.4 fusion.34
  181.0 1.6 collective-permute-start.4
  182.6 11.0 %collective-permute-done.10 = bf16[4,32,1792]{2,1,0:T(8,128)(2,1)S(1)} collective-permute-done((bf16[4,32,1792]{2,1,0:T(8,128)(2,1)S(1)}, bf16[4,32,1792]{2,1,0:T(8,128)(2,1)S(1)}, u32[]{:S(2)}, u32[]{:S(2)}) %collective-permute-start.10) | collective-permute-done | bytes 458784 | tf_op jit(solution)/shard_map/ppermute | solution.py:198
  193.8 1.7 collective-permute-start.11
  195.5 2.1 collective-permute-start.13
  198.3 4.1 %collective-permute-done.4 = bf16[4,32,1792]{2,1,0:T(8,128)(2,1)S(1)} collective-permute-done((bf16[4,32,1792]{2,1,0:T(8,128)(2,1)S(1)}, bf16[4,32,1792]{2,1,0:T(8,128)(2,1)S(1)}, u32[]{:S(2)}, u32[]{:S(2)}) %collective-permute-start.4) | collective-permute-done | bytes 458784 | tf_op jit(solution)/shard_map/ppermute | solution.py:198
  202.5 1.7 collective-permute-start.5
  204.3 2.1 collective-permute-start.7
  207.2 1.8 collective-permute-start.14
  209.0 1.6 collective-permute-done.5
  211.0 4.8 %collective-permute-done.6 = bf16[32,1792]{1,0:T(8,128)(2,1)S(1)} collective-permute-done((bf16[32,1792]{1,0:T(8,128)(2,1)S(1)}, bf16[32,1792]{1,0:T(8,128)(2,1)S(1)}, u32[]{:S(2)}, u32[]{:S(2)}) %collective-permute-start.6) | collective-permute-done | bytes 114720 | tf_op jit(solution)/shard_map/ppermute | solution.py:205
  215.9 1.6 collective-permute-start.8
  217.7 2.5 %collective-permute-done.8 = bf16[16,1792]{1,0:T(8,128)(2,1)S(1)} collective-permute-done((bf16[16,1792]{1,0:T(8,128)(2,1)S(1)}, bf16[16,1792]{1,0:T(8,128)(2,1)S(1)}, u32[]{:S(2)}, u32[]{:S(2)}) %collective-permute-start.8) | collective-permute-done | bytes 57376 | tf_op jit(solution)/shard_map/ppermute | solution.py:211
  (98 shorter events, 16.6 us)
Async XLA Ops:
  74.7 14.3 %slice-start = ((s8[7340032]{0:T(1024)(128)(4,1)}), s8[4194304]{0:T(1024)(128)(4,1)S(1)}, s32[]{:S(2)}) async-start(s8[7340032]{0:T(1024)(128)(4,1)} %bitcast.129), calls=%async_computation | async-start | bytes 8388608
  78.2 7.8 %copy-start.10 = (bf16[320,3584]{1,0:T(8,128)(2,1)}, bf16[320,3584]{1,0:T(8,128)(2,1)S(1)}, u32[]{:S(2)}) copy-start(bf16[320,3584]{1,0:T(8,128)(2,1)S(1)} %fusion.9) | copy-start | bytes 6881284
  78.2 9.3 %copy-start = (bf16[16,2,1,16,3584]{4,3,2,1,0:T(8,128)(2,1)S(1)}, bf16[16,2,1,16,3584]{4,3,2,1,0:T(8,128)(2,1)}, u32[]{:S(2)}) copy-start(bf16[16,2,1,16,3584]{4,3,2,1,0:T(8,128)(2,1)} %get-tuple-element.6) | copy-start | bytes 11010052
  78.3 10.7 %slice-start.1 = ((s8[7340032]{0:T(1024)(128)(4,1)}), s8[3145728]{0:T(1024)(128)(4,1)S(1)}, s32[]{:S(2)}) async-start(s8[7340032]{0:T(1024)(128)(4,1)} %bitcast.129), calls=%async_computation.1 | async-start | bytes 6291456
  86.1 17.9 %collective-permute-start = (bf16[320,1024]{1,0:T(8,128)(2,1)}, bf16[320,1024]{1,0:T(8,128)(2,1)}, u32[]{:S(2)}, u32[]{:S(2)}) collective-permute-start(bf16[320,1024]{1,0:T(8,128)(2,1)} %get-tuple-element.23), channel_id=1, source_target_pairs={{0,1},{1,0},{2,3},{3,2},{4,5},{5,4},{6,7},{7,6},{8,9},{9,8},{10,11... | collective-permute-start | bytes 1966088 | tf_op jit(solution)/shard_map/ppermute | solution.py:224
  87.6 5.4 %slice-start.4 = ((s8[7340032]{0:T(1024)(128)(4,1)}), s8[4194304]{0:T(1024)(128)(4,1)S(1)}, s32[]{:S(2)}) async-start(s8[7340032]{0:T(1024)(128)(4,1)} %bitcast.133), calls=%async_computation.4 | async-start | bytes 8388608
  89.0 3.9 %copy-start.8 = (bf16[320,3584]{1,0:T(8,128)(2,1)}, bf16[320,3584]{1,0:T(8,128)(2,1)S(1)}, u32[]{:S(2)}) copy-start(bf16[320,3584]{1,0:T(8,128)(2,1)S(1)} %convolution_convert_fusion.3) | copy-start | bytes 6881284
  89.0 3.9 %slice-start.5 = ((s8[7340032]{0:T(1024)(128)(4,1)}), s8[3145728]{0:T(1024)(128)(4,1)S(1)}, s32[]{:S(2)}) async-start(s8[7340032]{0:T(1024)(128)(4,1)} %bitcast.133), calls=%async_computation.5 | async-start | bytes 6291456
  92.4 25.5 %collective-permute-start.2 = (bf16[320,1024]{1,0:T(8,128)(2,1)}, bf16[320,1024]{1,0:T(8,128)(2,1)S(1)}, u32[]{:S(2)}, u32[]{:S(2)}) collective-permute-start(bf16[320,1024]{1,0:T(8,128)(2,1)} %get-tuple-element.25), channel_id=1, source_target_pairs={{0,1},{1,0},{2,3},{3,2},{4,5},{5,4},{6,7},{7,6},{8,9},{9,8},{10,11... | collective-permute-start | bytes 1966088 | tf_op jit(solution)/shard_map/ppermute | solution.py:224
  96.3 38.8 %copy-start.3 = (f32[320,1024]{1,0:T(8,128)}, f32[320,1024]{1,0:T(8,128)S(1)}, u32[]{:S(2)}) copy-start(f32[320,1024]{1,0:T(8,128)S(1)} %get-tuple-element.28) | copy-start | bytes 3932164
  96.3 35.2 %collective-permute-start.1 = (bf16[320,1024]{1,0:T(8,128)(2,1)}, bf16[320,1024]{1,0:T(8,128)(2,1)}, u32[]{:S(2)}, u32[]{:S(2)}) collective-permute-start(bf16[320,1024]{1,0:T(8,128)(2,1)} %get-tuple-element.27), channel_id=1, source_target_pairs={{0,1},{1,0},{2,3},{3,2},{4,5},{5,4},{6,7},{7,6},{8,9},{9,8},{10,11... | collective-permute-start | bytes 1966088 | tf_op jit(solution)/shard_map/ppermute | solution.py:224
  117.9 17.3 %copy-start.4 = (bf16[320,1024]{1,0:T(8,128)(2,1)}, bf16[320,1024]{1,0:T(8,128)(2,1)S(1)}, u32[]{:S(2)}) copy-start(bf16[320,1024]{1,0:T(8,128)(2,1)S(1)} %collective-permute-done.2) | copy-start | bytes 1966084
  131.5 8.7 %slice-start.2 = ((s8[7340032]{0:T(1024)(128)(4,1)}), s8[4194304]{0:T(1024)(128)(4,1)S(1)}, s32[]{:S(2)}) async-start(s8[7340032]{0:T(1024)(128)(4,1)} %bitcast.131), calls=%async_computation.2 | async-start | bytes 8388608
  135.1 5.1 %copy-start.5 = (bf16[320,1024]{1,0:T(8,128)(2,1)}, bf16[320,1024]{1,0:T(8,128)(2,1)S(1)}, u32[]{:S(2)}) copy-start(bf16[320,1024]{1,0:T(8,128)(2,1)S(1)} %get-tuple-element.9) | copy-start | bytes 1966084
  135.1 5.1 %slice-start.3 = ((s8[7340032]{0:T(1024)(128)(4,1)}), s8[3145728]{0:T(1024)(128)(4,1)S(1)}, s32[]{:S(2)}) async-start(s8[7340032]{0:T(1024)(128)(4,1)} %bitcast.131), calls=%async_computation.3 | async-start | bytes 6291456
  148.6 1.5 copy-start.1
  150.1 28.5 %collective-permute-start.9 = (bf16[4,2,32,1792]{3,2,1,0:T(8,128)(2,1)}, bf16[4,2,32,1792]{3,2,1,0:T(8,128)(2,1)}, u32[]{:S(2)}, u32[]{:S(2)}) collective-permute-start(bf16[4,2,32,1792]{3,2,1,0:T(8,128)(2,1)} %dynamic-slice_bitcast_fusion), channel_id=1, source_target_pairs={{0,2},{2,0},{4,6},{6,4},{8,10},{10,8},{12,14},{14,12},{16,18},{18,... | collective-permute-start | bytes 2752520 | tf_op jit(solution)/shard_map/ppermute | solution.py:194
  155.7 10.6 %copy-start.7 = (bf16[320,1024]{1,0:T(8,128)(2,1)S(1)}, bf16[320,1024]{1,0:T(8,128)(2,1)}, u32[]{:S(2)}) copy-start(bf16[320,1024]{1,0:T(8,128)(2,1)} %get-tuple-element.8) | copy-start | bytes 1966084
  155.7 10.6 %copy-start.9 = (bf16[320,3584]{1,0:T(8,128)(2,1)S(1)}, bf16[320,3584]{1,0:T(8,128)(2,1)}, u32[]{:S(2)}) copy-start(bf16[320,3584]{1,0:T(8,128)(2,1)} %copy-done.8) | copy-start | bytes 6881284
  155.7 25.1 %collective-permute-start.3 = (bf16[4,2,32,1792]{3,2,1,0:T(8,128)(2,1)S(1)}, bf16[4,2,32,1792]{3,2,1,0:T(8,128)(2,1)S(1)}, u32[]{:S(2)}, u32[]{:S(2)}) collective-permute-start(bf16[4,2,32,1792]{3,2,1,0:T(8,128)(2,1)S(1)} %dynamic-slice_bitcast_fusion.1), channel_id=1, source_target_pairs={{0,2},{2,0},{4,6},{6,4},{8,10},{10,8},{12,14},{14,12},{16,18},{18,... | collective-permute-start | bytes 2752520 | tf_op jit(solution)/shard_map/ppermute | solution.py:194
  166.3 6.3 %copy-start.6 = (bf16[320,1024]{1,0:T(8,128)(2,1)S(1)}, bf16[320,1024]{1,0:T(8,128)(2,1)}, u32[]{:S(2)}) copy-start(bf16[320,1024]{1,0:T(8,128)(2,1)} %copy-done.5) | copy-start | bytes 1966084
  172.6 6.1 %copy-start.2 = (bf16[512,1792]{1,0:T(8,128)(2,1)S(1)}, bf16[512,1792]{1,0:T(8,128)(2,1)}, u32[]{:S(2)}) copy-start(bf16[512,1792]{1,0:T(8,128)(2,1)} %copy-done.1) | copy-start | bytes 5505028
  180.2 13.5 %collective-permute-start.10 = (bf16[4,32,1792]{2,1,0:T(8,128)(2,1)S(1)}, bf16[4,32,1792]{2,1,0:T(8,128)(2,1)S(1)}, u32[]{:S(2)}, u32[]{:S(2)}) collective-permute-start(bf16[4,32,1792]{2,1,0:T(8,128)(2,1)S(1)} %dynamic-slice_bitcast_fusion.2), channel_id=1, source_target_pairs={{0,4},{2,6},{4,0},{6,2},{8,12},{10,14},{12,8},{14,10},{16,20},{18,... | collective-permute-start | bytes 1376264 | tf_op jit(solution)/shard_map/ppermute | solution.py:198
  181.0 21.3 %collective-permute-start.4 = (bf16[4,32,1792]{2,1,0:T(8,128)(2,1)S(1)}, bf16[4,32,1792]{2,1,0:T(8,128)(2,1)S(1)}, u32[]{:S(2)}, u32[]{:S(2)}) collective-permute-start(bf16[4,32,1792]{2,1,0:T(8,128)(2,1)S(1)} %dynamic-slice_bitcast_fusion.3), channel_id=1, source_target_pairs={{0,4},{2,6},{4,0},{6,2},{8,12},{10,14},{12,8},{14,10},{16,20},{18,... | collective-permute-start | bytes 1376264 | tf_op jit(solution)/shard_map/ppermute | solution.py:198
  193.8 12.6 %collective-permute-start.11 = (bf16[32,1792]{1,0:T(8,128)(2,1)S(1)}, bf16[32,1792]{1,0:T(8,128)(2,1)S(1)}, u32[]{:S(2)}, u32[]{:S(2)}) collective-permute-start(bf16[32,1792]{1,0:T(8,128)(2,1)S(1)} %get-tuple-element.13), channel_id=1, source_target_pairs={{0,8},{2,10},{4,12},{6,14},{8,16},{10,18},{12,20},{14,22},{16,24},... | collective-permute-start | bytes 344072 | tf_op jit(solution)/shard_map/ppermute | solution.py:205
  195.5 11.5 %collective-permute-start.13 = (bf16[32,1792]{1,0:T(8,128)(2,1)S(1)}, bf16[32,1792]{1,0:T(8,128)(2,1)S(1)}, u32[]{:S(2)}, u32[]{:S(2)}) collective-permute-start(bf16[32,1792]{1,0:T(8,128)(2,1)S(1)} %get-tuple-element.14), channel_id=1, source_target_pairs={{0,24},{2,26},{4,28},{6,30},{8,0},{10,2},{12,4},{14,6},{16,8},{18,... | collective-permute-start | bytes 344072 | tf_op jit(solution)/shard_map/ppermute | solution.py:205
  197.7 9.4 %collective-permute-start.12 = (bf16[32,1792]{1,0:T(8,128)(2,1)S(1)}, bf16[32,1792]{1,0:T(8,128)(2,1)S(1)}, u32[]{:S(2)}, u32[]{:S(2)}) collective-permute-start(bf16[32,1792]{1,0:T(8,128)(2,1)S(1)} %get-tuple-element.15), channel_id=1, source_target_pairs={{0,16},{2,18},{4,20},{6,22},{8,24},{10,26},{12,28},{14,30},{16,0},... | collective-permute-start | bytes 344072 | tf_op jit(solution)/shard_map/ppermute | solution.py:205
  202.5 8.0 %collective-permute-start.5 = (bf16[32,1792]{1,0:T(8,128)(2,1)S(1)}, bf16[32,1792]{1,0:T(8,128)(2,1)S(1)}, u32[]{:S(2)}, u32[]{:S(2)}) collective-permute-start(bf16[32,1792]{1,0:T(8,128)(2,1)S(1)} %get-tuple-element.10), channel_id=1, source_target_pairs={{0,8},{2,10},{4,12},{6,14},{8,16},{10,18},{12,20},{14,22},{16,24},... | collective-permute-start | bytes 344072 | tf_op jit(solution)/shard_map/ppermute | solution.py:205
  204.3 6.7 %collective-permute-start.7 = (bf16[32,1792]{1,0:T(8,128)(2,1)S(1)}, bf16[32,1792]{1,0:T(8,128)(2,1)S(1)}, u32[]{:S(2)}, u32[]{:S(2)}) collective-permute-start(bf16[32,1792]{1,0:T(8,128)(2,1)S(1)} %get-tuple-element.11), channel_id=1, source_target_pairs={{0,24},{2,26},{4,28},{6,30},{8,0},{10,2},{12,4},{14,6},{16,8},{18,... | collective-permute-start | bytes 344072 | tf_op jit(solution)/shard_map/ppermute | solution.py:205
  206.4 9.4 %collective-permute-start.6 = (bf16[32,1792]{1,0:T(8,128)(2,1)S(1)}, bf16[32,1792]{1,0:T(8,128)(2,1)S(1)}, u32[]{:S(2)}, u32[]{:S(2)}) collective-permute-start(bf16[32,1792]{1,0:T(8,128)(2,1)S(1)} %get-tuple-element.12), channel_id=1, source_target_pairs={{0,16},{2,18},{4,20},{6,22},{8,24},{10,26},{12,28},{14,30},{16,0},... | collective-permute-start | bytes 344072 | tf_op jit(solution)/shard_map/ppermute | solution.py:205
  207.2 10.4 %collective-permute-start.14 = (bf16[16,1792]{1,0:T(8,128)(2,1)S(1)}, bf16[16,1792]{1,0:T(8,128)(2,1)S(1)}, u32[]{:S(2)}, u32[]{:S(2)}) collective-permute-start(bf16[16,1792]{1,0:T(8,128)(2,1)S(1)} %get-tuple-element.18), channel_id=1, source_target_pairs={{0,1},{1,0},{2,3},{3,2},{4,5},{5,4},{6,7},{7,6},{8,9},{9,8},{10,11... | collective-permute-start | bytes 172040 | tf_op jit(solution)/shard_map/ppermute | solution.py:211
  215.9 4.2 %collective-permute-start.8 = (bf16[16,1792]{1,0:T(8,128)(2,1)S(1)}, bf16[16,1792]{1,0:T(8,128)(2,1)S(1)}, u32[]{:S(2)}, u32[]{:S(2)}) collective-permute-start(bf16[16,1792]{1,0:T(8,128)(2,1)S(1)} %get-tuple-element.16), channel_id=1, source_target_pairs={{0,1},{1,0},{2,3},{3,2},{4,5},{5,4},{6,7},{7,6},{8,9},{9,8},{10,11... | collective-permute-start | bytes 172040 | tf_op jit(solution)/shard_map/ppermute | solution.py:211
